TPU v7x, 32 devices: a whole 2x2x4 slice. The times are simulated.
32 devices in a mesh: wide: 16 (over z, x, core), lat: 2 (over y).
Axes of the slice: x: 2, y: 2, z: 4, core: 2. Of those that a mesh axis runs over, the one named last changes fastest.
Arguments:
- block_input: bfloat16 [16, 4, 641, 1152], P('wide', None, None, 'lat'), may hold values from -6 to 6
- noise_fields: bfloat16 [16, 4, 8, 1152], P('wide', None, None, 'lat'), may hold values from -6 to 6
- filter_taps: float32 [18, 3, 3, 5], P('lat'), may hold values from -1.5 to 1.5
- rollout: int32 [16], P('wide'), may hold values from 1 to 4
- cotangent: bfloat16 [16, 4, 641, 1152], P('wide', None, None, 'lat'), may hold values from -6 to 6
- params: bfloat16 [2897920], P('wide'), may hold values from -2 to 2, as said below
Outputs:
- block_output: bfloat16 [16, 4, 641, 1152], P('wide', None, None, 'lat')
- input_grad: float32 [16, 4, 641, 1152], P('wide', None, None, 'lat')
- param_grad: float32 [2897920], P('wide')
Inputs may be any that keep to these rules, and one draw needn't show every extreme that they name: `params`: entries from 2896679 on are padding.
All inputs are finite; a program needn't handle non-finite values.
Results may differ from a plain program's by a relative error of at most 0.0061.
Values may be sent and summed in bfloat16 or wider, within the bound.
A program may use at most 256 MiB of HBM per device.

v0:
```python
from functools import partial

import jax
import jax.numpy as jnp
from jax import lax
from jax.sharding import PartitionSpec as P

HID = 1282


def with_halo(cells, sides, width):
    for axis, dim in sides:
        count = lax.axis_size(axis)
        ends = count - 1
        head = lax.slice_in_dim(cells, 0, width, axis=dim)
        tail = lax.slice_in_dim(cells, cells.shape[dim] - width, cells.shape[dim], axis=dim)
        cells = jnp.concatenate(
            [
                lax.ppermute(tail, axis, [(i, (i + 1) % count) for i in range(ends)]),
                cells,
                lax.ppermute(head, axis, [((i + 1) % count, i) for i in range(ends)]),
            ],
            axis=dim,
        )
    return cells


def contract(left, right, left_dim, right_dim):
    return lax.dot_general(
        left, right, (((left_dim,), (right_dim,)), ((), ())), preferred_element_type=jnp.float32
    )


def norm_forward(values):
    centre = jnp.mean(values, 0)
    shifted = values - centre
    inv_scale = lax.rsqrt(jnp.mean(jnp.square(shifted), 0) + 1e-05)
    return (shifted * inv_scale, inv_scale)


def norm_backward(grad_normed, normed_hat, inv_scale, gain):
    scaled = grad_normed * gain[:, None]
    return inv_scale * (
        scaled - jnp.mean(scaled, 0) - normed_hat * jnp.mean(scaled * normed_hat, 0)
    )


def shards(block_input, noise_fields, filter_taps, rollout, cotangent, params):
    flat_params = lax.all_gather(params, "wide", axis=0, tiled=True)
    chans = block_input.shape[2]
    inputs = chans + noise_fields.shape[2]
    basis = filter_taps.shape[1]
    band_rows = filter_taps.shape[0]
    cells = block_input.shape[3]
    lon_count = cells // band_rows
    tap_count = filter_taps.shape[3]
    half_taps = tap_count // 2
    hidden_width = HID
    lengths = [
        chans,
        chans,
        chans * basis * inputs,
        chans,
        chans,
        chans,
        chans * hidden_width,
        hidden_width,
        hidden_width * chans,
        chans,
    ]
    pieces = []
    offset = 0
    for length in lengths:
        pieces.append(flat_params[offset : offset + length])
        offset = offset + length
    gain_one = pieces[0].astype(jnp.float32)
    bias_one = pieces[1].astype(jnp.float32)
    disco_weight = pieces[2].reshape(chans, basis * inputs)
    disco_bias = pieces[3].astype(jnp.float32)
    gain_two = pieces[4].astype(jnp.float32)
    bias_two = pieces[5].astype(jnp.float32)
    up_weight = pieces[6].reshape(chans, hidden_width)
    up_bias = pieces[7].astype(jnp.float32)
    down_weight = pieces[8].reshape(hidden_width, chans)
    down_bias = pieces[9].astype(jnp.float32)
    gelu_exact = partial(jax.nn.gelu, approximate=False)

    def step_pass(x_step, noise_step, cot_step, live_mask):
        x_values = x_step.astype(jnp.float32)
        hat_one, inv_one = norm_forward(x_values)
        normed_one = hat_one * gain_one[:, None] + bias_one[:, None]
        noisy = jnp.concatenate([normed_one.astype(jnp.bfloat16), noise_step], 0)
        noisy_grid = noisy.reshape(inputs, band_rows, lon_count)
        padded = with_halo(noisy_grid, (("lat", 1),), 1)
        basis_acc = jnp.zeros((basis, inputs, band_rows, lon_count), jnp.float32)
        for lat_off in range(3):
            rows = padded[:, lat_off : lat_off + band_rows, :].astype(jnp.float32)
            for lon_off in range(tap_count):
                moved = jnp.roll(rows, half_taps - lon_off, axis=2)
                coef = jnp.transpose(filter_taps[:, :, lat_off, lon_off])
                basis_acc = basis_acc + coef[:, None, :, None] * moved[None]
        basis_out = basis_acc.reshape(basis * inputs, cells).astype(jnp.bfloat16)
        disco = (
            jnp.dot(disco_weight, basis_out, preferred_element_type=jnp.float32)
            + disco_bias[:, None]
        )
        residual = x_values + disco
        hat_two, inv_two = norm_forward(residual)
        normed_two = (hat_two * gain_two[:, None] + bias_two[:, None]).astype(jnp.bfloat16)
        pre_act = contract(up_weight, normed_two, 0, 0) + up_bias[:, None]
        hidden_f, gelu_pull = jax.vjp(gelu_exact, pre_act)
        hidden = hidden_f.astype(jnp.bfloat16)
        branch = contract(down_weight, hidden, 0, 0) + down_bias[:, None]
        output_step = (live_mask * (residual + branch)).astype(jnp.bfloat16)
        grad_out = cot_step.astype(jnp.float32) * live_mask
        grad_low = grad_out.astype(jnp.bfloat16)
        grad_down = contract(hidden, grad_low, 1, 1)
        grad_down_bias = jnp.sum(grad_low.astype(jnp.float32), 1)
        grad_hidden = jnp.dot(down_weight, grad_low, preferred_element_type=jnp.float32)
        grad_pre = gelu_pull(grad_hidden)[0].astype(jnp.bfloat16)
        grad_up = contract(normed_two, grad_pre, 1, 1)
        grad_up_bias = jnp.sum(grad_pre.astype(jnp.float32), 1)
        grad_normed = jnp.dot(up_weight, grad_pre, preferred_element_type=jnp.float32)
        grad_gain_two = jnp.sum(grad_normed * hat_two, 1)
        grad_bias_two = jnp.sum(grad_normed, 1)
        grad_resid = grad_out + norm_backward(grad_normed, hat_two, inv_two, gain_two)
        grad_disco = grad_resid.astype(jnp.bfloat16)
        grad_disco_bias = jnp.sum(grad_disco.astype(jnp.float32), 1)
        grad_disco_weight = contract(grad_disco, basis_out, 1, 1)
        grad_basis = contract(disco_weight, grad_disco, 0, 0).reshape(
            basis, inputs, band_rows, lon_count
        )
        grad_padded = jnp.zeros((inputs, band_rows + 2, lon_count), jnp.float32)
        for lat_off in range(3):
            lat_sum = jnp.zeros((inputs, band_rows, lon_count), jnp.float32)
            for lon_off in range(tap_count):
                coef = jnp.transpose(filter_taps[:, :, lat_off, lon_off])
                weighted = jnp.sum(coef[:, None, :, None] * grad_basis, 0)
                lat_sum = lat_sum + jnp.roll(weighted, lon_off - half_taps, axis=2)
            grad_padded = grad_padded + jnp.pad(lat_sum, ((0, 0), (lat_off, 2 - lat_off), (0, 0)))
        rim_rows = jnp.concatenate(
            [grad_padded[:, 0:1, :], grad_padded[:, band_rows + 1 : band_rows + 2, :]], 1
        )
        arrived = with_halo(rim_rows.astype(jnp.bfloat16), (("lat", 1),), 1).astype(rim_rows.dtype)
        grad_noisy = grad_padded[:, 1 : band_rows + 1, :]
        grad_noisy = grad_noisy.at[:, 0, :].add(arrived[:, 0, :])
        grad_noisy = grad_noisy.at[:, band_rows - 1, :].add(arrived[:, 3, :])
        grad_first = grad_noisy[:chans].reshape(chans, cells)
        grad_gain_one = jnp.sum(grad_first * hat_one, 1)
        grad_bias_one = jnp.sum(grad_first, 1)
        input_step = grad_resid + norm_backward(grad_first, hat_one, inv_one, gain_one)
        grads = (
            grad_gain_one,
            grad_bias_one,
            grad_disco_weight,
            grad_disco_bias,
            grad_gain_two,
            grad_bias_two,
            grad_up,
            grad_up_bias,
            grad_down,
            grad_down_bias,
        )
        return (output_step, input_step, grads)

    grad_start = (
        jnp.zeros((chans,), jnp.float32),
        jnp.zeros((chans,), jnp.float32),
        jnp.zeros((chans, basis * inputs), jnp.float32),
        jnp.zeros((chans,), jnp.float32),
        jnp.zeros((chans,), jnp.float32),
        jnp.zeros((chans,), jnp.float32),
        jnp.zeros((chans, hidden_width), jnp.float32),
        jnp.zeros((hidden_width,), jnp.float32),
        jnp.zeros((hidden_width, chans), jnp.float32),
        jnp.zeros((chans,), jnp.float32),
    )
    dates = block_input.shape[0]
    step_total = block_input.shape[1]
    step_ids = jnp.arange(step_total, dtype=jnp.int32)
    live = (step_ids[None, :] < rollout[:, None]).astype(jnp.float32).reshape(dates * step_total)
    x_items = block_input.reshape(dates * step_total, chans, cells)
    noise_items = noise_fields.reshape(dates * step_total, noise_fields.shape[2], cells)
    cot_items = cotangent.reshape(dates * step_total, chans, cells)

    def scan_step(grad_total, item_data):
        x_item, noise_item, cot_item, mask_item = item_data
        output_step, input_step, grads = step_pass(x_item, noise_item, cot_item, mask_item)
        summed = tuple((total + part for total, part in zip(grad_total, grads)))
        return (summed, (output_step, input_step))

    grad_total, (outputs, inputs_grad) = lax.scan(
        scan_step, grad_start, (x_items, noise_items, cot_items, live)
    )
    block_output = outputs.reshape(block_input.shape)
    input_grad = inputs_grad.reshape(block_input.shape)
    padded_total = params.shape[0] * lax.axis_size("wide")
    flat_grad = jnp.concatenate(
        [part.reshape(-1) for part in grad_total]
        + [jnp.zeros((padded_total - offset,), jnp.float32)]
    )
    band_total = lax.psum(flat_grad, "lat")
    param_grad = lax.psum_scatter(band_total, "wide", scatter_dimension=0, tiled=True)
    return (block_output, input_grad, param_grad)


def solution(mesh):
    in_specs = (
        P("wide", None, None, "lat"),
        P("wide", None, None, "lat"),
        P("lat", None, None, None),
        P("wide"),
        P("wide", None, None, "lat"),
        P("wide"),
    )
    out_specs = (P("wide", None, None, "lat"), P("wide", None, None, "lat"), P("wide"))
    return jax.shard_map(shards, mesh=mesh, in_specs=in_specs, out_specs=out_specs, check_vma=False)
```

profile of v0, /device:TPU:0, one launch (start us, length us, event | category | flops | bytes accessed | tf_op | source)
XLA Modules:
  0.0 1748.4 jit_solution(16056616127928051996)
XLA Ops:
  19.7 90.1 %all-gather.3.cloned.1.call-done = bf16[16,1,181120]{2,1,0:T(2,128)(2,1)} async-done(((bf16[1,1,181120]{2,1,0:T(2,128)(2,1)}), bf16[16,1,181120]{2,1,0:T(2,128)(2,1)}) %all-gather.3.cloned.1.call-update) | async-done | bytes 5795856 | tf_op jit(solution)/shard_map/all_gather | solution.py:49
  109.8 122.9 %reduce.20 = bf16[16,181120]{1,0:T(8,128)(2,1)} reduce(bf16[16,1,181120]{2,1,0:T(2,128)(2,1)} %all-gather.3.cloned.1.call-done, bf16[]{:T(256)} %constant.304), dimensions={1}, to_apply=%all-gather.reduce_sub_computation | reduce | bytes 11591682 | tf_op jit(solution)/shard_map/all_gather | solution.py:49
  232.7 12.0 reshape.478
  273.4 1095.3 %while.37 = (s32[]{:T(128)}, f32[641]{0:T(1024)}, f32[641]{0:T(1024)}, f32[641,1947]{1,0:T(8,128)}, f32[641]{0:T(1024)}, /*index=5*/f32[641]{0:T(1024)}, f32[641...) while((s32[]{:T(128)}, f32[641]{0:T(1024)}, ...), condition=%wide.region_31.32_spmd.clone, body=%wide.region_0.31_spmd.clone.sunk | while | flops 10174124032 | bytes 555897216 | solution.py:192
  311.2 16.6 add_convert_fusion.10
  364.0 10.1 reshape.492
  374.2 76.7 %multiply_reduce_fusion.27 = (f32[649,9,64]{0,2,1:T(8,128)}, f32[649,9,64]{0,2,1:T(8,128)}, f32[649,9,64]{0,2,1:T(8,128)}, f32[649,9,64]{0,2,1:T(8,128)}, f32[64...) fusion(f32[3,649,9,64]{1,0,3,2:T(4,128)} %reshape.492, ...), kind=kLoop, calls=%fused_computation.11.clone.1 | loop fusion | flops 28036800 | bytes 26916948 | tf_op jit(solution)/shard_map/while/body/eval_jaxpr/reduce_sum | solution.py:138
  512.4 31.6 %dynamic_update_slice.20 = f32[4,641,576]{2,0,1:T(4,128)} dynamic-update-slice(f32[4,641,576]{2,0,1:T(4,128)} %get-tuple-element.1113, f32[1,641,576]{2,0,1:T(1,128)S(1)} %copy.136, s32[]{:T(128)S(6)} %copy.154, s32[]{:T(128)} %constant.286.clone.1..sunk, s32[]{:T(128)} %constant.286.clone.1..sunk) | dynamic-update-slice | bytes 2953732 | tf_op jit(solution)/shard_map/while/body/jit(dynamic_update_index_in_dim)/dynamic_update_slice | solution.py:192
  580.2 16.6 add_convert_fusion.10
  633.2 10.1 reshape.492
  643.4 76.4 %multiply_reduce_fusion.27 = (f32[649,9,64]{0,2,1:T(8,128)}, f32[649,9,64]{0,2,1:T(8,128)}, f32[649,9,64]{0,2,1:T(8,128)}, f32[649,9,64]{0,2,1:T(8,128)}, f32[64...) fusion(f32[3,649,9,64]{1,0,3,2:T(4,128)} %reshape.492, ...), kind=kLoop, calls=%fused_computation.11.clone.1 | loop fusion | flops 28036800 | bytes 26916948 | tf_op jit(solution)/shard_map/while/body/eval_jaxpr/reduce_sum | solution.py:138
  784.3 31.6 %dynamic_update_slice.20 = f32[4,641,576]{2,0,1:T(4,128)} dynamic-update-slice(f32[4,641,576]{2,0,1:T(4,128)} %get-tuple-element.1113, f32[1,641,576]{2,0,1:T(1,128)S(1)} %copy.136, s32[]{:T(128)S(6)} %copy.154, s32[]{:T(128)} %constant.286.clone.1..sunk, s32[]{:T(128)} %constant.286.clone.1..sunk) | dynamic-update-slice | bytes 2953732 | tf_op jit(solution)/shard_map/while/body/jit(dynamic_update_index_in_dim)/dynamic_update_slice | solution.py:192
  852.0 16.6 add_convert_fusion.10
  904.9 10.1 reshape.492
  915.1 76.6 %multiply_reduce_fusion.27 = (f32[649,9,64]{0,2,1:T(8,128)}, f32[649,9,64]{0,2,1:T(8,128)}, f32[649,9,64]{0,2,1:T(8,128)}, f32[649,9,64]{0,2,1:T(8,128)}, f32[64...) fusion(f32[3,649,9,64]{1,0,3,2:T(4,128)} %reshape.492, ...), kind=kLoop, calls=%fused_computation.11.clone.1 | loop fusion | flops 28036800 | bytes 26916948 | tf_op jit(solution)/shard_map/while/body/eval_jaxpr/reduce_sum | solution.py:138
  1055.9 31.6 %dynamic_update_slice.20 = f32[4,641,576]{2,0,1:T(4,128)} dynamic-update-slice(f32[4,641,576]{2,0,1:T(4,128)} %get-tuple-element.1113, f32[1,641,576]{2,0,1:T(1,128)S(1)} %copy.136, s32[]{:T(128)S(6)} %copy.154, s32[]{:T(128)} %constant.286.clone.1..sunk, s32[]{:T(128)} %constant.286.clone.1..sunk) | dynamic-update-slice | bytes 2953732 | tf_op jit(solution)/shard_map/while/body/jit(dynamic_update_index_in_dim)/dynamic_update_slice | solution.py:192
  1123.9 16.6 add_convert_fusion.10
  1153.6 9.6 fusion.144
  1176.6 10.1 reshape.492
  1186.9 76.7 %multiply_reduce_fusion.27 = (f32[649,9,64]{0,2,1:T(8,128)}, f32[649,9,64]{0,2,1:T(8,128)}, f32[649,9,64]{0,2,1:T(8,128)}, f32[649,9,64]{0,2,1:T(8,128)}, f32[64...) fusion(f32[3,649,9,64]{1,0,3,2:T(4,128)} %reshape.492, ...), kind=kLoop, calls=%fused_computation.11.clone.1 | loop fusion | flops 28036800 | bytes 26916948 | tf_op jit(solution)/shard_map/while/body/eval_jaxpr/reduce_sum | solution.py:138
  1327.8 31.6 %dynamic_update_slice.20 = f32[4,641,576]{2,0,1:T(4,128)} dynamic-update-slice(f32[4,641,576]{2,0,1:T(4,128)} %get-tuple-element.1113, f32[1,641,576]{2,0,1:T(1,128)S(1)} %copy.136, s32[]{:T(128)S(6)} %copy.154, s32[]{:T(128)} %constant.286.clone.1..sunk, s32[]{:T(128)} %constant.286.clone.1..sunk) | dynamic-update-slice | bytes 2953732 | tf_op jit(solution)/shard_map/while/body/jit(dynamic_update_index_in_dim)/dynamic_update_slice | solution.py:192
  1392.3 95.8 %concatenate.198 = f32[2897920]{0:T(1024)} concatenate(f32[641]{0:T(1024)S(1)} %copy-done.106, f32[641]{0:T(1024)S(1)} %copy-done.103, f32[1248027]{0:T(1024)} %reshape.465, f32[641]{0:T(1024)S(1)} %copy-done.100, f32[641]{0:T(1024)S(1)} %copy-done.97, f32[641]{0:T(1024)S(1)} %copy-done.94, f32[821762]{0:T(1024)} %reshape.466, f32[1282]{0:T(1024)S(1)} %copy-done.85, ...), dimensions={0} | concatenate | bytes 23183360 | tf_op jit(solution)/shard_map/concatenate | solution.py:198
  1490.0 213.5 %all-reduce.9.cloned.1.call-done = f32[2897920]{0:T(1024)} async-done(((f32[2897920]{0:T(1024)}), f32[2897920]{0:T(1024)}) %all-reduce.9.cloned.1.call-update) | async-done | bytes 11591696
  1708.7 30.8 %all-reduce.7.cloned.1.call-done = f32[181120]{0:T(1024)} async-done(((f32[181120]{0:T(1024)}), f32[181120]{0:T(1024)}) %all-reduce.7.cloned.1.call-update) | async-done | bytes 724496 | tf_op jit(solution)/shard_map/psum | solution.py:202
  (1387 shorter events, 602.2 us)
Async XLA Ops:
  7.2 102.6 %all-gather.3.cloned.1.call-start = ((), (), s32[]{:S(2)}) async-start(), calls=%async_computation.1 | async-start | bytes 12316160 | tf_op jit(solution)/shard_map/all_gather | solution.py:49
  12.3 1691.1 %all-reduce.9.cloned.1.call-start = ((), (), s32[]{:S(2)}) async-start(), calls=%async_computation.2 | async-start | bytes 23183360
  273.9 83.4 %copy-start.107 = (f32[641]{0:T(1024)}, f32[641]{0:T(1024)S(1)}, u32[]{:S(2)}) copy-start(f32[641]{0:T(1024)S(1)} %get-tuple-element.1154) | copy-start | bytes 7696 | tf_op jit(solution)/shard_map/while
  281.9 15.6 collective-permute-start
  285.3 12.2 collective-permute-start.1
  489.1 15.5 collective-permute-start.2
  490.6 13.9 collective-permute-start.3
  544.9 81.5 %copy-start.107 = (f32[641]{0:T(1024)}, f32[641]{0:T(1024)S(1)}, u32[]{:S(2)}) copy-start(f32[641]{0:T(1024)S(1)} %get-tuple-element.1154) | copy-start | bytes 7696 | tf_op jit(solution)/shard_map/while
  553.0 13.5 collective-permute-start
  554.3 12.2 collective-permute-start.1
  760.7 15.7 collective-permute-start.2
  762.2 14.2 collective-permute-start.3
  816.8 81.4 %copy-start.107 = (f32[641]{0:T(1024)}, f32[641]{0:T(1024)S(1)}, u32[]{:S(2)}) copy-start(f32[641]{0:T(1024)S(1)} %get-tuple-element.1154) | copy-start | bytes 7696 | tf_op jit(solution)/shard_map/while
  824.8 13.5 collective-permute-start
  826.1 12.2 collective-permute-start.1
  1032.6 15.5 collective-permute-start.2
  1034.1 13.9 collective-permute-start.3
  1088.6 81.3 %copy-start.107 = (f32[641]{0:T(1024)}, f32[641]{0:T(1024)S(1)}, u32[]{:S(2)}) copy-start(f32[641]{0:T(1024)S(1)} %get-tuple-element.1154) | copy-start | bytes 7696 | tf_op jit(solution)/shard_map/while
  1096.7 13.5 collective-permute-start
  1098.0 12.2 collective-permute-start.1
  1304.4 15.5 collective-permute-start.2
  1306.0 13.9 collective-permute-start.3
  1488.1 217.6 %copy-start.34 = (bf16[4,641,576]{2,1,0:T(8,128)(2,1)S(1)}, bf16[4,641,576]{2,1,0:T(8,128)(2,1)}, u32[]{:S(2)}) copy-start(bf16[4,641,576]{2,1,0:T(8,128)(2,1)} %get-tuple-element.382) | copy-start | bytes 8861188
  1488.1 251.3 %all-reduce.7.cloned.1.call-start = ((), (), s32[]{:S(2)}) async-start(), calls=%async_computation | async-start | bytes 1449984 | tf_op jit(solution)/shard_map/psum | solution.py:202
  (438 other events, 2987.5 us)
Sparse Core Ops, SparseCore 0:
  12.4 97.3 all-gather.2
  1488.2 215.1 all-reduce.8
  1706.3 33.0 all-reduce.6
where the time goes:
time: 1770 us; the launch traced here: 1750 us
  other arithmetic  603 us (34%)
  local copies, waits for them, and re-layouts  552 us (31%)
  waiting for transfers between devices  334 us (19%)
  matrix products  188 us (11%)
  starting transfers between devices  38.5 us (2%)
    reduce_sum x4, other arithmetic, step_pass(): weighted = jnp.sum(coef[:, None, :, None] * grad_basis, 0)  306 us
    unnamed x4, waiting for transfers between devices  214 us
    dot_general x24, matrix products, contract(): lax.dot_general(left, right, (((left_dim,), (right_dim,)), ((), ())), pre...  141 us
    dynamic_update_slice x8, local copies, waits for them, and re-layouts, shards(): lax.scan(scan_step, grad_start, (x_items, noise_items, cot_items, live))  133 us
    all_gather x1, other arithmetic, shards(): flat_params = lax.all_gather(params, 'wide', axis=0, tiled=True)  123 us
    concatenate x1, local copies, waits for them, and re-layouts, shards(): jnp.concatenate([part.reshape(-1) for part in grad_total] + [jnp.zeros((p...  95.8 us
    all_gather x1, waiting for transfers between devices, shards(): flat_params = lax.all_gather(params, 'wide', axis=0, tiled=True)  90.1 us
    convert_element_type x4, other arithmetic, step_pass(): basis_out = basis_acc.reshape(basis * inputs, cells).astype(jnp.bfloat16)  66.4 us
  transfers between devices with their start and end apart: 19, of which 3 were waited for; matrix products, arithmetic and copies ran while one was open for 5% of the time, Pallas kernels for 0%

commit v1 on v0

v1 whole, which is shorter than its diff:
```python
from functools import partial

import jax
import jax.numpy as jnp
from jax import lax
from jax.experimental import pallas as pl
from jax.experimental.pallas import tpu as pltpu
from jax.sharding import PartitionSpec as P

HID = 1282
BF = jnp.bfloat16
F32 = jnp.float32
EPS = 1e-05
NEAR = 256
MESH = pl.DeviceIdType.MESH


def up_to(size, unit):
    return -(-size // unit) * unit


def mm(left, right, dims=(1, 0)):
    return lax.dot_general(
        left, right, (((dims[0],), (dims[1],)), ((), ())), preferred_element_type=F32
    )


class Sizes:
    def __init__(self, block_input, noise_fields, filter_taps):
        self.steps = block_input.shape[0] * block_input.shape[1]
        self.chans = block_input.shape[2]
        self.noise = noise_fields.shape[2]
        self.inputs = self.chans + self.noise
        self.rows = filter_taps.shape[0]
        self.basis = filter_taps.shape[1]
        self.taps = filter_taps.shape[3]
        self.cells = block_input.shape[3]
        self.lons = self.cells // self.rows
        self.chan_pad = up_to(self.inputs + 1, 16)
        self.chan_main = self.chans // 128 * 128
        self.rest = self.chan_pad - self.chan_main
        self.hid = HID
        self.hid_pad = up_to(HID + 1, 16)
        self.mix = self.basis * self.chan_pad
        self.main = (self.rows - 1) * self.lons
        self.width = self.steps * self.cells
        self.tail = self.steps * self.main


def block_kernel(
    sz, x_hbm, noise_ref, cot_hbm, halo_ref, taps_ref, live_ref, norm_ref, mix_hbm, mixt_hbm,
    up_hbm, down_hbm, out_hbm, grad_hbm, dmix_hbm, dup_hbm, ddown_hbm, dnorm_ref,
    xs, gs, basis_s, normed_s, act_s, gd_s, grad_s, stage, noisy_s, filt_s, filt_e,
    edge_s, mix_s, up_s, down_s,
    in_sem, w_sem, out_sem, send_sem, recv_sem,
):
    chans, cp, cm, rest = sz.chans, sz.chan_pad, sz.chan_main, sz.rest
    hp, lons, main, tail = sz.hid_pad, sz.lons, sz.main, sz.tail
    pair = 2 * lons
    lat = lax.axis_index("lat")
    lat_count = lax.axis_size("lat")
    has_up = lat > 0
    has_down = lat < lat_count - 1

    def fetch(step, slot):
        return (
            pltpu.make_async_copy(x_hbm.at[step], stage.at[slot], in_sem.at[slot, 0]),
            pltpu.make_async_copy(cot_hbm.at[step], stage.at[2 + slot], in_sem.at[slot, 1]),
        )

    for step in range(2):
        for copy in fetch(step, step):
            copy.start()
    weights = [
        pltpu.make_async_copy(src, dst, w_sem.at[i])
        for i, (src, dst) in enumerate(((mix_hbm, mix_s), (up_hbm, up_s), (down_hbm, down_s)))
    ]
    for copy in weights:
        copy.start()
    mixt_s = normed_s.at[:, pl.ds(0, mixt_hbm.shape[1])]
    mixt_copy = pltpu.make_async_copy(mixt_hbm, mixt_s, w_sem.at[3])

    row_in = lax.broadcasted_iota(jnp.int32, (lons, pair), 0)
    lane = lax.broadcasted_iota(jnp.int32, (lons, pair), 1)
    lane_in = lane % lons
    left_half = lane < lons
    half_taps = sz.taps // 2
    circ = []
    circ_t = []
    for t in range(sz.taps):
        circ.append(row_in == (lane_in + (t - half_taps + lons)) % lons)
        circ_t.append(lane_in == (row_in + (t - half_taps + lons)) % lons)
    tap_stride = sz.basis * 3 * sz.taps

    def tap_block(ext_row_a, a_a, ext_row_b, a_b, k, masks):
        block = jnp.zeros((lons, pair), F32)
        for t in range(sz.taps):
            va = F32(0) if a_a is None else taps_ref[ext_row_a * tap_stride + (k * 3 + a_a) * sz.taps + t]
            vb = F32(0) if a_b is None else taps_ref[ext_row_b * tap_stride + (k * 3 + a_b) * sz.taps + t]
            block = jnp.where(masks[t], jnp.where(left_half, va, vb), block)
        return block.astype(BF)

    def inside(a):
        return a if 0 <= a <= 2 else None

    windows = (sz.rows - 1) // 2
    last = sz.rows - 1

    def build_filters(backward):
        def build(index, _):
            m = index // sz.basis
            k = index % sz.basis
            cols = pl.ds(pl.multiple_of(k * pair, pair), pair)
            for ri in range(4):
                if backward:
                    block = tap_block(
                        2 * m + ri, inside(2 - ri), 2 * m + ri, inside(3 - ri), k, circ_t
                    )
                else:
                    block = tap_block(
                        2 * m + 1, inside(ri), 2 * m + 2, inside(ri - 1), k, circ
                    )
                filt_s[m, pl.ds(ri * lons, lons), cols] = block
            return 0

        def build_last(k, _):
            cols = pl.ds(pl.multiple_of(k * pair, pair), pair)
            for ri in range(4):
                ext = min(last + ri, last + 2) if backward else last + 1
                a = inside(2 - ri) if backward else inside(ri)
                masks = circ_t if backward else circ
                for odd in range(2):
                    filt_e[pl.ds((odd * 4 + ri) * lons, lons), cols] = tap_block(
                        ext, None if odd else a, ext, a if odd else None, k, masks
                    )
            return 0

        lax.fori_loop(0, windows * sz.basis, build, 0)
        lax.fori_loop(0, sz.basis, build_last, 0)

    build_filters(False)

    gain_one, bias_one = norm_ref[0], norm_ref[1]
    gain_two, bias_two = norm_ref[2], norm_ref[3]

    def wide(vec, lanes):
        if lanes <= 128:
            return vec[:, :lanes]
        return jnp.concatenate([vec] * (lanes // 128) + ([vec[:, : lanes % 128]] if lanes % 128 else []), 1)

    def stats(values):
        centre = jnp.sum(values, 0, keepdims=True) * (1.0 / chans)
        shifted = values - centre
        spread = jnp.sum(jnp.square(shifted), 0, keepdims=True) * (1.0 / chans)
        return shifted, lax.rsqrt(spread + EPS)

    def norm_one(values, lanes):
        shifted, inv = stats(values)
        return shifted * inv * wide(gain_one[:chans], lanes) + wide(bias_one[:chans], lanes)

    halos = []
    for side, there in ((0, has_up), (1, has_down)):
        fields = halo_ref[side].astype(F32)
        width = fields.shape[1]
        normed = norm_one(fields[:chans], width)
        noise = fields[chans : sz.inputs]
        full = jnp.concatenate(
            [normed, noise, jnp.zeros((cp - sz.inputs, width), F32)], 0
        )
        edge_s[side] = jnp.where(there, full, 0.0).astype(BF)

    def halo_part(source, step):
        return source[:, step * lons : (step + 1) * lons]

    ones_row = (lax.broadcasted_iota(jnp.int32, (rest, pair), 0) == sz.inputs - cm).astype(F32)

    def run_filter(slot, store):
        for m in range(windows):
            window = noisy_s[slot, :, m * pair : m * pair + 2 * pair]
            result = mm(window, filt_s[m])
            for k in range(sz.basis):
                store(m, k, result[:, k * pair : (k + 1) * pair])

    def run_last(store):
        window = jnp.concatenate(
            [noisy_s[slot, :, windows * pair : windows * pair + 2 * pair] for slot in range(2)], 1
        )
        result = mm(window, filt_e[...])
        for k in range(sz.basis):
            store(k, result[:, k * pair : (k + 1) * pair])

    def put_basis(lanes, k, part, ones):
        basis_s[k * cm : (k + 1) * cm, lanes] = part[:cm].astype(BF)
        low = part[cm:]
        if ones and k == 0:
            low = low + ones_row
        start = sz.basis * cm + k * rest
        basis_s[start : start + rest, lanes] = low.astype(BF)

    zero_lanes = jnp.zeros((cp, lons), BF)
    pad_rows = jnp.zeros((cp - chans, sz.cells), F32)
    pad_pair = jnp.zeros((cp - chans, pair), F32)
    pairs = sz.steps // 2

    def prepare(two, _):
        both = pl.ds(pl.multiple_of(tail + two * pair, pair), pair)
        near = pl.ds(pl.multiple_of(two * pair, pair), pair)
        for slot in range(2):
            step = 2 * two + slot
            for copy in fetch(step, slot):
                copy.wait()
            fields = stage[slot].astype(F32)
            normed = norm_one(fields, sz.cells)
            noise = noise_ref[step].astype(F32)
            own = jnp.concatenate(
                [normed, noise, jnp.zeros((cp - sz.inputs, sz.cells), F32)], 0
            ).astype(BF)
            noisy_s[slot] = jnp.concatenate(
                [
                    halo_part(edge_s[0, :, near], slot),
                    own,
                    halo_part(edge_s[1, :, near], slot),
                    zero_lanes,
                ],
                1,
            )
            lanes = pl.ds(pl.multiple_of(step * main, main), main)
            xs[:, lanes] = jnp.concatenate([fields, pad_rows], 0)[:, :main].astype(BF)
            masked = jnp.concatenate([stage[2 + slot].astype(F32), pad_rows], 0)[:, :main]
            gs[:, lanes] = (masked * live_ref[:, lanes]).astype(BF)

            def keep(m, k, part, step=step):
                start = pl.multiple_of(step * main + m * pair, pair)
                put_basis(pl.ds(start, pair), k, part, True)

            run_filter(slot, keep)
        x_tail = jnp.concatenate([stage[s, :, main:] for s in range(2)], 1).astype(F32)
        xs[:, both] = jnp.concatenate([x_tail, pad_pair], 0).astype(BF)
        g_tail = jnp.concatenate([stage[2 + s, :, main:] for s in range(2)], 1).astype(F32)
        g_tail = jnp.concatenate([g_tail, pad_pair], 0)
        gs[:, both] = (g_tail * live_ref[:, both]).astype(BF)
        run_last(lambda k, part: put_basis(both, k, part, True))

        @pl.when(two + 1 < pairs)
        def _():
            for slot in range(2):
                for copy in fetch(2 * two + 2 + slot, slot):
                    copy.start()

        return 0

    lax.fori_loop(0, pairs, prepare, 0)
    barrier = pltpu.get_barrier_semaphore()

    @pl.when(has_up)
    def _():
        pl.semaphore_signal(barrier, inc=1, device_id={"lat": lat - 1}, device_id_type=MESH)

    @pl.when(has_down)
    def _():
        pl.semaphore_signal(barrier, inc=1, device_id={"lat": lat + 1}, device_id_type=MESH)

    for copy in weights:
        copy.wait()
    dnorm_ref[...] = jnp.zeros_like(dnorm_ref)

    def fold(values):
        total = values[:, :128]
        for i in range(1, values.shape[1] // 128):
            total = total + values[:, i * 128 : (i + 1) * 128]
        return total

    chunks = sz.width // NEAR
    per_step = main // NEAR
    tail_chunk = tail // NEAR
    steps_per_tail = NEAR // lons

    def split_store(chunk, put):
        @pl.when(chunk < tail_chunk)
        def _():
            start = pl.multiple_of((chunk % per_step) * NEAR, NEAR)
            put(chunk // per_step, pl.ds(start, NEAR), slice(0, NEAR))

        @pl.when(chunk >= tail_chunk)
        def _():
            for part in range(steps_per_tail):
                put(
                    (chunk - tail_chunk) * steps_per_tail + part,
                    pl.ds(main, lons),
                    slice(part * lons, (part + 1) * lons),
                )

    def out_copy(step):
        return pltpu.make_async_copy(stage.at[step], out_hbm.at[step], out_sem.at[0, step])

    def grad_copy(step):
        return pltpu.make_async_copy(grad_s.at[step], grad_hbm.at[step], out_sem.at[1, step])

    tail_total = chunks - tail_chunk

    def forward_chunk(index, _):
        chunk = lax.rem(index + tail_chunk, chunks)
        lanes = pl.ds(pl.multiple_of(chunk * NEAR, NEAR), NEAR)
        residual = xs[:, lanes].astype(F32) + mm(mix_s[:, : sz.mix], basis_s[:, lanes])
        centre = jnp.sum(residual[:chans], 0, keepdims=True) * (1.0 / chans)
        shifted = residual - centre
        spread = jnp.sum(jnp.square(shifted[:chans]), 0, keepdims=True) * (1.0 / chans)
        inv = lax.rsqrt(spread + EPS)
        hat = shifted * inv
        normed = (hat * wide(gain_two, NEAR) + wide(bias_two, NEAR)).astype(BF)
        normed_s[:, lanes] = normed
        grad_low = gs[:, lanes]
        pre = mm(up_s[:, :hp], normed, (0, 0))
        grad_hidden = mm(down_s[:, :cp], grad_low)
        phi = 0.5 + 0.5 * lax.erf(pre * 0.7071067811865476)
        density = jnp.exp(pre * pre * -0.5) * 0.3989422804014327
        hidden = pre * phi
        grad_pre = (grad_hidden * (phi + pre * density)).astype(BF)
        low_rows = hp - HID // 16 * 16
        low = lax.broadcasted_iota(jnp.int32, (low_rows, NEAR), 0) == HID - (hp - low_rows)
        hidden = jnp.concatenate(
            [hidden[: hp - low_rows], jnp.where(low, 1.0, hidden[hp - low_rows :])], 0
        ).astype(BF)
        act_s[:hp, lanes] = hidden
        act_s[hp:, lanes] = grad_pre
        branch = mm(down_s[:, :cp], hidden, (0, 0))
        output = ((residual + branch)[:chans] * live_ref[:, lanes]).astype(BF)

        def put_out(step, where, part):
            stage[step, :, where] = output[:, part]

        split_store(chunk, put_out)

        grad_normed = mm(up_s[:, :hp], grad_pre)
        dnorm_ref[2] += fold(grad_normed * hat)
        dnorm_ref[3] += fold(grad_normed)
        scaled = grad_normed * wide(gain_two, NEAR)
        mean_one = jnp.sum(scaled[:chans], 0, keepdims=True) * (1.0 / chans)
        mean_two = jnp.sum((scaled * hat)[:chans], 0, keepdims=True) * (1.0 / chans)
        grad_resid = grad_low.astype(F32) + inv * (scaled - mean_one - hat * mean_two)
        gd_s[:, lanes] = grad_resid.astype(BF)

        def put_grad(step, where, part):
            grad_s[step, :, where] = grad_resid[:chans, part]

        split_store(chunk, put_grad)

        @pl.when((chunk < tail_chunk) & (lax.rem(chunk, per_step) == per_step - 1))
        def _():
            out_copy(chunk // per_step).start()

        return 0

    lax.fori_loop(0, chunks, forward_chunk, 0)

    rim = pl.ds(0, sz.steps * lons)
    noisy_s[0, :, rim] = jnp.concatenate(
        [gd_s[:, step * main : step * main + lons] for step in range(sz.steps)], 1
    )
    noisy_s[1, :, rim] = gd_s[:, tail:]
    pl.semaphore_wait(barrier, has_up.astype(jnp.int32) + has_down.astype(jnp.int32))

    def send(side, to):
        return pltpu.make_async_remote_copy(
            src_ref=noisy_s.at[side, :, rim],
            dst_ref=edge_s.at[1 - side],
            send_sem=send_sem.at[side],
            recv_sem=recv_sem.at[1 - side],
            device_id={"lat": to},
            device_id_type=MESH,
        )

    @pl.when(has_up)
    def _():
        send(0, lat - 1).start()

    @pl.when(has_down)
    def _():
        send(1, lat + 1).start()

    def blocks(total, size):
        return [(i, min(size, total - i)) for i in range(0, total, size)]

    for start, size in blocks(hp, 512):
        up_s[:, start : start + size] = mm(
            normed_s[...], act_s[hp + start : hp + start + size, :], (1, 1)
        ).astype(BF)
    dup_copy = pltpu.make_async_copy(up_s, dup_hbm, w_sem.at[1])
    dup_copy.start()
    mixt_copy.start()
    for start, size in blocks(hp, 432):
        rows = pl.ds(start, size)
        down_s[rows, :cp] = mm(act_s[rows, :], gs[...], (1, 1)).astype(BF)
    ddown_copy = pltpu.make_async_copy(down_s, ddown_hbm, w_sem.at[2])
    ddown_copy.start()
    for start, size in blocks(sz.mix, 512):
        mix_s[:, start : start + size] = mm(
            gd_s[...], basis_s[start : start + size, :], (1, 1)
        ).astype(BF)
    dmix_copy = pltpu.make_async_copy(mix_s, dmix_hbm, w_sem.at[0])
    dmix_copy.start()

    build_filters(True)

    @pl.when(has_up)
    def _():
        send(0, lat - 1).wait_send()
        send(1, lat - 1).wait_recv()

    @pl.when(has_down)
    def _():
        send(1, lat + 1).wait_send()
        send(0, lat + 1).wait_recv()

    def adjoint(two, _):
        both = pl.ds(pl.multiple_of(tail + two * pair, pair), pair)
        near = pl.ds(pl.multiple_of(two * pair, pair), pair)
        for slot in range(2):
            step = 2 * two + slot
            noisy_s[slot] = jnp.concatenate(
                [
                    halo_part(edge_s[0, :, near], slot),
                    gd_s[:, pl.ds(pl.multiple_of(step * main, main), main)],
                    halo_part(gd_s[:, both], slot),
                    halo_part(edge_s[1, :, near], slot),
                    zero_lanes,
                ],
                1,
            )

            def keep_grad(m, k, part, step=step):
                start = pl.multiple_of(step * main + m * pair, pair)
                put_basis(pl.ds(start, pair), k, part, False)

            run_filter(slot, keep_grad)
        run_last(lambda k, part: put_basis(both, k, part, False))
        return 0

    lax.fori_loop(0, pairs, adjoint, 0)
    mixt_copy.wait()

    def backward_chunk(index, _):
        chunk = lax.rem(index + tail_chunk, chunks)
        lanes = pl.ds(pl.multiple_of(chunk * NEAR, NEAR), NEAR)
        grad_first = mm(normed_s[:, : sz.mix], basis_s[:, lanes])[:chans]
        shifted, inv = stats(xs[:, lanes].astype(F32)[:chans])
        hat = shifted * inv
        dnorm_ref[0, :chans] += fold(grad_first * hat)
        dnorm_ref[1, :chans] += fold(grad_first)
        scaled = grad_first * wide(gain_one[:chans], NEAR)
        mean_one = jnp.sum(scaled, 0, keepdims=True) * (1.0 / chans)
        mean_two = jnp.sum(scaled * hat, 0, keepdims=True) * (1.0 / chans)
        added = inv * (scaled - mean_one - hat * mean_two)

        def put_grad(step, where, part):
            grad_s[step, :, where] += added[:, part]

        split_store(chunk, put_grad)

        @pl.when((chunk < tail_chunk) & (lax.rem(chunk, per_step) == per_step - 1))
        def _():
            grad_copy(chunk // per_step).start()

        return 0

    lax.fori_loop(0, chunks, backward_chunk, 0)
    for step in range(sz.steps):
        out_copy(step).wait()
        grad_copy(step).wait()
    for copy in (ddown_copy, dup_copy, dmix_copy):
        copy.wait()


def shift_rows(values, axis, down):
    count = lax.axis_size(axis)
    if down:
        pairs = [(i, i + 1) for i in range(count - 1)]
    else:
        pairs = [(i + 1, i) for i in range(count - 1)]
    return lax.ppermute(values, axis, pairs)


def run_block(sz, x_items, noise_items, cot_items, filter_taps, live, norms, mix, mixt, up, down):
    cp, hp = sz.chan_pad, sz.hid_pad
    lons = sz.lons

    def edge(first):
        lanes = slice(0, lons) if first else slice(sz.cells - lons, sz.cells)
        rows = jnp.concatenate([x_items[:, :, lanes], noise_items[:, :, lanes]], 1)
        rows = jnp.transpose(rows, (1, 0, 2)).reshape(sz.inputs, sz.steps * lons)
        return jnp.pad(rows, ((0, cp - sz.inputs), (0, 0)))

    halo = jnp.stack([shift_rows(edge(False), "lat", True), shift_rows(edge(True), "lat", False)])
    taps_ext = jnp.concatenate(
        [
            shift_rows(filter_taps[-1:], "lat", True),
            filter_taps,
            shift_rows(filter_taps[:1], "lat", False),
        ],
        0,
    ).reshape(-1)
    live_lanes = jnp.concatenate([jnp.repeat(live, sz.main), jnp.repeat(live, lons)])[None]
    any_spec = pl.BlockSpec(memory_space=pl.ANY)
    vmem = pl.BlockSpec(memory_space=pltpu.VMEM)
    mix_lanes = up_to(sz.mix, 128)
    up_lanes = up_to(hp, 128)
    down_lanes = up_to(cp, 128)
    windows = (sz.rows - 1) // 2
    lon = lons
    flops = 2 * sz.width * (3 * sz.mix * cp + 6 * hp * cp)
    return pl.pallas_call(
        partial(block_kernel, sz),
        name="block",
        out_shape=[
            jax.ShapeDtypeStruct(x_items.shape, BF),
            jax.ShapeDtypeStruct(x_items.shape, F32),
            jax.ShapeDtypeStruct((cp, mix_lanes), BF),
            jax.ShapeDtypeStruct((cp, up_lanes), BF),
            jax.ShapeDtypeStruct((hp, down_lanes), BF),
            jax.ShapeDtypeStruct((4, cp, 128), F32),
        ],
        in_specs=[
            any_spec, vmem, any_spec, vmem, pl.BlockSpec(memory_space=pltpu.SMEM), vmem, vmem,
            any_spec, any_spec, any_spec, any_spec,
        ],
        out_specs=[any_spec] * 5 + [vmem],
        scratch_shapes=[
            pltpu.VMEM((cp, sz.width), BF),
            pltpu.VMEM((cp, sz.width), BF),
            pltpu.VMEM((sz.mix, sz.width), BF),
            pltpu.VMEM((cp, sz.width), BF),
            pltpu.VMEM((2 * hp, sz.width), BF),
            pltpu.VMEM((cp, sz.width), BF),
            pltpu.VMEM((sz.steps, sz.chans, sz.cells), F32),
            pltpu.VMEM((4, sz.chans, sz.cells), BF),
            pltpu.VMEM((2, cp, (sz.rows + 3) * lon), BF),
            pltpu.VMEM((windows, 4 * lon, sz.basis * 2 * lon), BF),
            pltpu.VMEM((8 * lon, sz.basis * 2 * lon), BF),
            pltpu.VMEM((2, cp, sz.steps * lon), BF),
            pltpu.VMEM((cp, mix_lanes), BF),
            pltpu.VMEM((cp, up_lanes), BF),
            pltpu.VMEM((hp, down_lanes), BF),
            pltpu.SemaphoreType.DMA((2, 2)),
            pltpu.SemaphoreType.DMA((4,)),
            pltpu.SemaphoreType.DMA((2, sz.steps)),
            pltpu.SemaphoreType.DMA((2,)),
            pltpu.SemaphoreType.DMA((2,)),
        ],
        compiler_params=pltpu.CompilerParams(
            collective_id=0, has_side_effects=True, vmem_limit_bytes=63 * 1024 * 1024
        ),
        cost_estimate=pl.CostEstimate(flops=flops, bytes_accessed=40_000_000, transcendentals=0),
    )(x_items, noise_items, cot_items, halo, taps_ext, live_lanes, norms, mix, mixt, up, down)


def unpack(sz, flat):
    chans, hid, inputs, basis = sz.chans, sz.hid, sz.inputs, sz.basis
    cm, rest, cp, hp = sz.chan_main, sz.rest, sz.chan_pad, sz.hid_pad
    lengths = [chans, chans, chans * basis * inputs, chans, chans, chans, chans * hid, hid,
               hid * chans, chans]
    pieces = []
    offset = 0
    for length in lengths:
        pieces.append(flat[offset : offset + length])
        offset = offset + length

    def column(vec, ones=None):
        vec = jnp.pad(vec.astype(F32), (0, cp - chans))
        if ones is not None:
            vec = vec.at[ones].set(1.0)
        return jnp.broadcast_to(vec[:, None], (cp, 128))

    norms = jnp.stack(
        [column(pieces[0]), column(pieces[1]), column(pieces[4]), column(pieces[5], chans)]
    )
    disco = pieces[2].reshape(chans, basis, inputs)

    def packed(values, bias):
        values = jnp.pad(values, ((0, cp - values.shape[0]), (0, 0), (0, cp - values.shape[2])))
        head = values[:, :, :cm].reshape(cp, basis * cm)
        low = values[:, :, cm:].reshape(cp, basis * rest)
        if bias is not None:
            low = low.at[:chans, inputs - cm].set(bias)
        full = jnp.concatenate([head, low], 1)
        return jnp.pad(full, ((0, 0), (0, up_to(full.shape[1], 128) - full.shape[1])))

    mix = packed(disco, pieces[3])
    mixt = packed(jnp.transpose(disco, (2, 1, 0))[:chans], None)
    up = pieces[6].reshape(chans, hid)
    up = jnp.concatenate([up, pieces[7][None]], 0)
    up = jnp.pad(up, ((0, cp - chans - 1), (0, up_to(hp, 128) - hid)))
    down = jnp.concatenate([pieces[8].reshape(hid, chans), pieces[9][None]], 0)
    down = jnp.pad(down, ((0, hp - hid - 1), (0, up_to(cp, 128) - chans)))
    return norms, mix, mixt, up, down


def shards(block_input, noise_fields, filter_taps, rollout, cotangent, params):
    sz = Sizes(block_input, noise_fields, filter_taps)
    chans, cm, rest = sz.chans, sz.chan_main, sz.rest
    flat = lax.all_gather(params, "wide", axis=0, tiled=True)
    norms, mix, mixt, up, down = unpack(sz, flat)
    dates, step_total = block_input.shape[:2]
    step_ids = jnp.arange(step_total, dtype=jnp.int32)
    live = (step_ids[None, :] < rollout[:, None]).astype(F32).reshape(sz.steps)
    items = (sz.steps, chans, sz.cells)
    out, grad, dmix, dup, ddown, dnorm = run_block(
        sz,
        block_input.reshape(items),
        noise_fields.reshape(sz.steps, sz.noise, sz.cells),
        cotangent.reshape(items),
        filter_taps,
        live,
        norms,
        mix,
        mixt,
        up,
        down,
    )
    dvec = jnp.sum(dnorm, 2).astype(BF)[:, :chans]
    low = dmix[:chans, sz.basis * cm : sz.mix].reshape(chans, sz.basis, rest)
    ddisco = jnp.concatenate(
        [dmix[:chans, : sz.basis * cm].reshape(chans, sz.basis, cm), low[:, :, : sz.inputs - cm]], 2
    )
    parts = [
        dvec[0], dvec[1], ddisco, low[:, 0, sz.inputs - cm], dvec[2], dvec[3],
        dup[:chans, :HID], dup[chans, :HID], ddown[:HID, :chans], ddown[HID, :chans],
    ]
    padded = params.shape[0] * lax.axis_size("wide")
    parts = [part.reshape(-1) for part in parts]
    used = sum(part.shape[0] for part in parts)
    flat_grad = jnp.concatenate(parts + [jnp.zeros((padded - used,), BF)])
    mine = lax.psum_scatter(flat_grad, "wide", scatter_dimension=0, tiled=True)
    param_grad = lax.psum(mine.astype(F32), "lat")
    return (out.reshape(block_input.shape), grad.reshape(block_input.shape), param_grad)


def solution(mesh):
    in_specs = (
        P("wide", None, None, "lat"),
        P("wide", None, None, "lat"),
        P("lat", None, None, None),
        P("wide"),
        P("wide", None, None, "lat"),
        P("wide"),
    )
    out_specs = (P("wide", None, None, "lat"), P("wide", None, None, "lat"), P("wide"))
    return jax.shard_map(shards, mesh=mesh, in_specs=in_specs, out_specs=out_specs, check_vma=False)
```

time: 1770 us -> 723 us (0.41)
  other arithmetic: 603 us -> 145 us
  local copies, waits for them, and re-layouts: 552 us -> 232 us
  matrix products: 188 us -> 0 us
  waiting for transfers between devices: 334 us -> 211 us
  Pallas kernels: 0 us -> 94.3 us
  starting transfers between devices: 38.5 us -> 13.7 us
    reduce_sum x28 -> x1, other arithmetic: 345 us -> 1.81 us  [shards(): dvec = jnp.sum(dnorm, 2).astype(BF)[:, :chans]]
    dot_general x36 -> x0, matrix products: 188 us -> none  [the longest x24 141 us: contract(): lax.dot_general(left, right, (((left_dim,), (right_dim,)), ((), ())), pre...]
    dynamic_update_slice x8 -> x0, local copies, waits for them, and re-layouts: 133 us -> none  [shards(): lax.scan(scan_step, grad_start, (x_items, noise_items, cot_items, live))]
    pallas_call x0 -> x1, Pallas kernels: none -> 94.3 us  [run_block(): pl.pallas_call(partial(block_kernel, sz), name='block', out_shape=[jax.Sh...]
    unnamed x4, waiting for transfers between devices: 214 us -> 129 us
    convert_element_type x19 -> x2, other arithmetic: 78.3 us -> 2.08 us  [the longest x1 2.07 us: shards(): param_grad = lax.psum(mine.astype(F32), 'lat')]
    while x866 -> x0, local copies, waits for them, and re-layouts: 52.8 us -> none
    reshape x15 -> x14, local copies, waits for them, and re-layouts: 91.6 us -> 52.4 us  [the longest x3 17.1 us: shards(): parts = [part.reshape(-1) for part in parts]]
  transfers between devices with their start and end apart: 19 -> 7, of which waited for: 3 -> 3; matrix products, arithmetic and copies ran while one was open for 5% -> 5% of each run, Pallas kernels for 0% -> 0%
where the time goes in v1:
time: 723 us; the launch traced here: 712 us
  local copies, waits for them, and re-layouts  232 us (32%)
  waiting for transfers between devices  211 us (29%)
  other arithmetic  145 us (20%)
  Pallas kernels  94.3 us (13%)
  between operations  15.5 us (2%)
  starting transfers between devices  13.7 us (2%)
    unnamed x4, waiting for transfers between devices  129 us
    all_gather x1, other arithmetic, shards(): flat = lax.all_gather(params, 'wide', axis=0, tiled=True)  123 us
    pallas_call x1, Pallas kernels, run_block(): pl.pallas_call(partial(block_kernel, sz), name='block', out_shape=[jax.Sh...  94.3 us
    concatenate x1, local copies, waits for them, and re-layouts, shards(): flat_grad = jnp.concatenate(parts + [jnp.zeros((padded - used,), BF)])  86.2 us
    all_gather x1, waiting for transfers between devices, shards(): flat = lax.all_gather(params, 'wide', axis=0, tiled=True)  59.3 us
    unnamed x40, local copies, waits for them, and re-layouts  36.3 us
    psum x1, waiting for transfers between devices, shards(): param_grad = lax.psum(mine.astype(F32), 'lat')  23.3 us
    reshape x3, local copies, waits for them, and re-layouts, shards(): parts = [part.reshape(-1) for part in parts]  17.1 us
  transfers between devices with their start and end apart: 7, of which 3 were waited for; matrix products, arithmetic and copies ran while one was open for 5% of the time, Pallas kernels for 0%

profile of v1, /device:TPU:0, one launch (start us, length us, event | category | flops | bytes accessed | tf_op | source)
XLA Modules:
  0.0 712.4 jit_solution(6348583703951230130)
XLA Ops:
  7.2 5.1 reshape.174
  23.0 5.6 collective-permute-start
  35.7 5.3 collective-permute-start.2
  50.5 59.3 %all-gather.3.cloned.1.call-done = bf16[16,1,181120]{2,1,0:T(2,128)(2,1)} async-done(((bf16[1,1,181120]{2,1,0:T(2,128)(2,1)}), bf16[16,1,181120]{2,1,0:T(2,128)(2,1)}) %all-gather.3.cloned.1.call-update) | async-done | bytes 5795856 | tf_op jit(solution)/shard_map/all_gather | solution.py:600
  109.8 123.0 %reduce.9 = bf16[16,181120]{1,0:T(8,128)(2,1)} reduce(bf16[16,1,181120]{2,1,0:T(2,128)(2,1)} %all-gather.3.cloned.1.call-done, bf16[]{:T(256)} %constant.95), dimensions={1}, to_apply=%all-gather.reduce_sub_computation | reduce | bytes 11591682 | tf_op jit(solution)/shard_map/all_gather | solution.py:600
  232.8 12.1 %reshape.175 = bf16[2897920]{0:T(1024)(128)(2,1)} reshape(bf16[16,181120]{1,0:T(8,128)(2,1)} %reduce.9) | data formatting | bytes 11591680
  248.6 8.0 %reshape.157 = bf16[641,3,649]{2,1,0:T(4,128)(2,1)} reshape(bf16[1248027]{0:T(1024)(128)(2,1)S(1)} %slice.180) | data formatting | bytes 4992108 | tf_op jit(solution)/shard_map/reshape | solution.py:576
  259.1 3.7 pad_slice_fusion.3
  265.0 3.2 fusion.19
  277.5 4.1 copy.52
  281.6 4.4 copy.54
  289.2 5.6 copy.46
  294.8 3.3 copy.51
  298.7 6.5 reshape.166
  305.2 5.8 reshape.165
  321.3 94.3 %block.1 = (bf16[4,641,576]{2,1,0:T(8,128)(2,1)}, f32[4,641,576]{2,1,0:T(8,128)}, bf16[656,2048]{1,0:T(8,128)(2,1)}, bf16[656,1408]{1,0:T(8,128)(2,1)}, bf16[129...) custom-call(bf16[4,641,576]{2,1,0:T(8,128)(2,1)} %bitcast.43, bf16[4,8,576]{2,1,0:T(8,128)(2,1)} %bitcast.54, ...), custom_call_target="tpu_custom_call" | custom-call | flops 41352560640 | bytes 40000000 | tf_op jit(solution)/shard_map/block/pallas_call | solution.py:511
  426.6 5.5 copy.58
  432.1 7.0 reshape.171
  439.0 5.2 reshape.173
  444.2 4.9 reshape.172
  451.0 86.2 %concatenate.43 = bf16[2897920]{0:T(1024)(128)(2,1)} concatenate(bf16[641]{0:T(1024)(128)(2,1)S(1)} %get-tuple-element.51, bf16[641]{0:T(1024)(128)(2,1)S(1)} %get-tuple-element.50, bf16[1248027]{0:T(1024)(128)(2,1)S(1)} %reshape.171, bf16[641]{0:T(1024)(128)(2,1)S(1)} %slice_reduce_fusion.3, bf16[641]{0:T(1024)(128)(2,1)S(1)} %get-tuple-element.49, ...), dimensions={0} | concatenate | bytes 11591680 | tf_op jit(solution)/shard_map/concatenate | solution.py:631
  539.1 128.6 %all-reduce.17.cloned.1.call-done = bf16[2897920]{0:T(1024)(128)(2,1)} async-done(((bf16[2897920]{0:T(1024)(128)(2,1)}), bf16[2897920]{0:T(1024)(128)(2,1)}) %all-reduce.17.cloned.1.call-update) | async-done | bytes 5795856
  669.8 7.5 %copy.60 = f32[1,4,641,576]{3,1,2,0:T(4,128)} copy(f32[1,4,641,576]{3,2,1,0:T(8,128)} %bitcast.41) | data formatting | bytes 11814912
  680.3 23.3 %all-reduce.15.cloned.1.call-done = f32[181120]{0:T(1024)} async-done(((f32[181120]{0:T(1024)}), f32[181120]{0:T(1024)}) %all-reduce.15.cloned.1.call-update) | async-done | bytes 724496 | tf_op jit(solution)/shard_map/psum | solution.py:633
  (112 shorter events, 79.4 us)
Async XLA Ops:
  7.2 102.6 %all-gather.3.cloned.1.call-start = ((), (), s32[]{:S(2)}) async-start(), calls=%async_computation.1 | async-start | bytes 12316160 | tf_op jit(solution)/shard_map/all_gather | solution.py:600
  12.3 655.4 %all-reduce.17.cloned.1.call-start = ((), (), s32[]{:S(2)}) async-start(), calls=%async_computation.2 | async-start | bytes 11591680
  14.7 2.4 copy-start.3
  17.1 18.6 %copy-start.9 = (f32[9,3,3,5]{0,2,3,1:T(4,128)S(1)}, f32[9,3,3,5]{0,2,3,1:T(4,128)}, u32[]{:S(2)}) copy-start(f32[9,3,3,5]{0,2,3,1:T(4,128)} %param.12) | copy-start | bytes 4864
  17.1 26.3 %copy-start.12 = (s32[2]{0:T(128)S(1)}, s32[2]{0:T(128)}, u32[]{:S(2)}) copy-start(s32[2]{0:T(128)} %constant.61.clone.1) | copy-start | bytes 28
  17.1 28.2 %copy-start.5 = (bf16[1,4,641,576]{3,1,2,0:T(4,128)(2,1)S(1)}, bf16[1,4,641,576]{3,1,2,0:T(4,128)(2,1)}, u32[]{:S(2)}) copy-start(bf16[1,4,641,576]{3,1,2,0:T(4,128)(2,1)} %param.14) | copy-start | bytes 8861188
  23.0 25.5 %collective-permute-start = (bf16[656,256]{1,0:T(8,128)(2,1)}, bf16[656,256]{1,0:T(8,128)(2,1)}, u32[]{:S(2)}, u32[]{:S(2)}) collective-permute-start(bf16[656,256]{1,0:T(8,128)(2,1)} %pad.60), channel_id=1, source_target_pairs={{0,1},{2,3},{4,5},{6,7},{8,9},{10,11},{12,13},{14,15},{16,17},{18,... | collective-permute-start | bytes 1007624 | tf_op jit(solution)/shard_map/ppermute | solution.py:480
  34.3 14.1 %collective-permute-start.1 = (bf16[656,256]{1,0:T(8,128)(2,1)}, bf16[656,256]{1,0:T(8,128)(2,1)}, u32[]{:S(2)}, u32[]{:S(2)}) collective-permute-start(bf16[656,256]{1,0:T(8,128)(2,1)} %pad.61), channel_id=1, source_target_pairs={{1,0},{3,2},{5,4},{7,6},{9,8},{11,10},{13,12},{15,14},{17,16},{19,... | collective-permute-start | bytes 1007624 | tf_op jit(solution)/shard_map/ppermute | solution.py:480
  35.7 11.7 %collective-permute-start.2 = (f32[1,3,3,5]{0,2,3,1:T(4,128)S(1)}, f32[1,3,3,5]{0,2,3,1:T(4,128)S(1)}, u32[]{:S(2)}, u32[]{:S(2)}) collective-permute-start(f32[1,3,3,5]{0,2,3,1:T(4,128)S(1)} %get-tuple-element.63), channel_id=1, source_target_pairs={{0,1},{2,3},{4,5},{6,7},{8,9},{10,11},{12,13},{14,15},{16,17},{18,... | collective-permute-start | bytes 548 | tf_op jit(solution)/shard_map/ppermute | solution.py:480
  41.0 6.4 collective-permute-start.3
  256.7 2.4 copy-start
  259.1 5.8 slice-start
  262.8 2.1 slice-start.1
  294.8 3.3 copy-start.10
  311.0 3.2 copy-start.2
  314.2 2.4 copy-start.1
  314.2 2.4 copy-start.8
  415.6 3.1 copy-start.7
  417.6 2.5 copy-start.6
  537.2 0.7 copy-start.11
  537.2 166.5 %all-reduce.15.cloned.1.call-start = ((), (), s32[]{:S(2)}) async-start(), calls=%async_computation | async-start | bytes 1449984 | tf_op jit(solution)/shard_map/psum | solution.py:633
  669.8 7.5 %copy-start.4 = (bf16[4,641,576]{2,1,0:T(8,128)(2,1)S(1)}, bf16[4,641,576]{2,1,0:T(8,128)(2,1)}, u32[]{:S(2)}) copy-start(bf16[4,641,576]{2,1,0:T(8,128)(2,1)} %get-tuple-element.33) | copy-start | bytes 8861188
Sparse Core Ops, SparseCore 0:
  12.4 97.3 all-gather.2
  537.3 130.3 all-reduce.16
  670.6 33.0 all-reduce.14
